TPU v7x, 32 devices: a whole 2x2x4 slice. The times are simulated.
32 devices in a mesh: img: 4 (over y, core), row: 8 (over z, x).
Axes of the slice: x: 2, y: 2, z: 4, core: 2. Of those that a mesh axis runs over, the one named last changes fastest.
Arguments:
- image_small: float32 [16, 32, 1024], P('img', 'row'), may hold values from -6 to 6
- image_large: float32 [12, 64, 2048], P('img', 'row'), may hold values from -6 to 6
- teacher_small: float32 [16, 32, 32], P('img', 'row'), may hold values from 0 to 0.0625
- teacher_large: float32 [12, 64, 64], P('img', 'row'), may hold values from 0 to 0.03125
- upstream_small: float32 [16, 32, 1024], P('img', 'row'), may hold values from -1.2 to 1.2
- upstream_large: float32 [12, 64, 2048], P('img', 'row'), may hold values from -1.2 to 1.2
- conv_first: float32 [3, 3, 32, 32], replicated, may hold values from -0.375 to 0.375
- gain_first: float32 [32], replicated, may hold values from 0.1 to 1.9
- bias_first: float32 [32], replicated, may hold values from -3 to 3
- conv_second: float32 [3, 3, 32, 32], replicated, may hold values from -0.375 to 0.375
- gain_second: float32 [32], replicated, may hold values from 0.1 to 1.9
- bias_second: float32 [32], replicated, may hold values from -3 to 3
Outputs:
- out_small: float32 [16, 32, 1024], P('img', 'row')
- out_large: float32 [12, 64, 2048], P('img', 'row')
- back_small: float32 [16, 32, 1024], P('img', 'row')
- back_large: float32 [12, 64, 2048], P('img', 'row')
- first_conv_grad: float32 [3, 3, 32, 32], replicated
- first_gain_grad: float32 [32], replicated
- first_bias_grad: float32 [32], replicated
- second_conv_grad: float32 [3, 3, 32, 32], replicated
- second_gain_grad: float32 [32], replicated
- second_bias_grad: float32 [32], replicated
All inputs are finite; a program needn't handle non-finite values.
Results may differ from a plain program's by a relative error of at most 0.0003.
Values sent between devices are 32-bit elements; how exact they have to be, the bound alone decides.
No kernel may reach another device: no remote copies, remote signals or barrier semaphores. Data moves between devices by JAX's collectives and lax.ppermute only.
A program may use at most 64 MiB of HBM per device.

v0:
```python
import functools
import math

import jax
import jax.numpy as jnp
from jax import lax
from jax.experimental import pallas as pl
from jax.experimental.pallas import tpu as pltpu
from jax.sharding import PartitionSpec as P

C = 32
HS = 32
HL = 64
HEIGHTS = (HS, HL)

norm_eps = 1e-05
map_eps = 1e-06
beta_weight = 1000.0
AXES = ("img", "row")
BLOCK = 8
LANES = BLOCK * C
TAPS = 3
DEPTH = TAPS * 128 + 256
TAP_ROWS = 128 + 2 * C
REACH = 4
ROOT = math.sqrt(2.0 / math.pi)
CUBE = 0.044715
F32 = jnp.float32
BF16 = jnp.bfloat16
VMEM_LIMIT = 32 * 1024 * 1024
BIAS, GAIN, SECOND, LEFT, HIDDEN, ONES = 0, 1, 2, 11, 20, 29
BACK_LANES = 1280
LAST_SECOND, LAST_FIRST, LAST_LANES = 2, 11, 640


class Sizes:
    def __init__(self, small, large, devices, peers):
        self.images = (small[0], large[0])
        self.rows = (small[1], large[1])
        self.blocks = (HS // BLOCK, HL // BLOCK)
        self.step = tuple(n * r for n, r in zip(self.images, self.rows))
        self.count = tuple(b * s for b, s in zip(self.blocks, self.step))
        self.edge = tuple(b * n for b, n in zip(self.blocks, self.images))
        self.start = (self.count[1], 0)
        self.rim = (self.edge[1], 0)
        self.total = sum(self.count)
        self.rims = sum(self.edge)
        self.slots = -(-sum(self.images) // 8) * 8
        self.guard = -(-max(self.images) // 8) * 8
        self.devices = devices
        self.peers = peers
        self.here = float(self.total * BLOCK)
        self.pixels = self.here * devices

    def pads(self):
        return [((TAPS, 2, self.count[k] + 2 * self.step[k], 128), F32) for k in (0, 1)]

    def chains(self, depth):
        return [((2, 2 * self.guard + (depth + 1) * self.rims, 128), F32)] * 2


def split(value):
    high = value.astype(BF16)
    return high, (value - high.astype(F32)).astype(BF16)


def dot(left, right):
    return lax.dot_general(left, right, (((1,), (0,)), ((), ())), preferred_element_type=F32)


def product(left, right):
    if left[0].shape[1] % 128:
        return dot(left[0], right[0]) + (dot(left[0], right[1]) + dot(left[1], right[0]))
    return dot(
        jnp.concatenate([left[0], left[0], left[1]], axis=1), jnp.concatenate([right[0], right[1], right[0]], axis=0)
    )


def spread(left, right):
    right = right.astype(BF16)
    return dot(jnp.concatenate(split(left), axis=1), jnp.concatenate([right, right], axis=0))


def gelu(s):
    return 0.5 * s * (1.0 + jnp.tanh(ROOT * (s + CUBE * s * s * s)))


def gelu_slope(s):
    square = s * s
    t = jnp.tanh(ROOT * s * (1.0 + CUBE * square))
    return 0.5 * (1.0 + t) + 0.5 * s * (1.0 - t * t) * ROOT * (1.0 + 3.0 * CUBE * square)


def spread_groups(row):
    row = row + pltpu.roll(row, 64, 1)
    return row + pltpu.roll(row, 32, 1)


def fold(row):
    return spread_groups(row[:, :128] + row[:, 128:])


def wide(row):
    return jnp.concatenate([row, row], axis=1)


def group_of(rows=1, lanes=128):
    return lax.broadcasted_iota(jnp.int32, (rows, lanes), 1) // C


def column_sum(value):
    return jnp.sum(value, axis=0, keepdims=True)


def send_lines(z, ref, lines):
    for n, line in enumerate(lines):
        ref[pl.ds(n, z.devices, stride=len(lines)), :] = jnp.broadcast_to(line, (z.devices, 128))


def moments(z, value, ref):
    few = min(8, z.total)
    pivot = fold(column_sum(value[:few])) / float(few * BLOCK)
    off = value - wide(pivot)
    first, second = fold(column_sum(off)), fold(column_sum(off * off))
    send_lines(z, ref, [pivot + first / z.here, second - first * first / z.here])


def merged(z, ref):
    means = ref[pl.ds(0, z.devices, stride=2), :]
    center = jnp.mean(means, axis=0, keepdims=True)
    off = means - center
    within = jnp.mean(ref[pl.ds(1, z.devices, stride=2), :], axis=0, keepdims=True)
    variance = within / z.here + jnp.mean(off * off, axis=0, keepdims=True)
    return wide(center), wide(lax.rsqrt(variance + norm_eps))


def put_halves(ref, value):
    ref[0] = value[:, :128]
    ref[1] = value[:, 128:]


def whole(ref):
    return jnp.concatenate([ref[0], ref[1]], axis=1)


def to_matrix(z, refs, half):
    for k in (0, 1):
        for j in range(z.blocks[k]):
            at = z.start[k] + j * z.step[k]
            for i in range(z.images[k]):
                for h in (0, 1):
                    half[h, pl.ds(at + i * z.rows[k], z.rows[k]), :] = refs[k][i, :, pl.ds(LANES * j + 128 * h, 128)]


def from_matrix(z, half, refs):
    for k in (0, 1):
        for j in range(z.blocks[k]):
            at = z.start[k] + j * z.step[k]
            for i in range(z.images[k]):
                for h in (0, 1):
                    refs[k][i, :, pl.ds(LANES * j + 128 * h, 128)] = half[h, pl.ds(at + i * z.rows[k], z.rows[k]), :]


def is_even():
    return lax.axis_index("row") % 2 == 0


def put_edges(pair, other, at, last, first):
    even = is_even()
    pair[at] = jnp.where(even, last, first)
    other[at] = jnp.where(even, first, last)


def above_of(pair, other, at):
    return jnp.where(is_even(), other[at], pair[at])


def below_of(pair, other, at):
    return jnp.where(is_even(), pair[at], other[at])


def take_rims(z, half, depth, pair, other):
    everything = pl.ds(0, 128)
    for k in (0, 1):
        nothing = jnp.zeros((z.edge[k], 128), F32)
        for n in range(depth):
            first, last = nothing, nothing
            if depth - n <= z.rows[k]:
                last = half[pl.ds(z.start[k] + z.rows[k] - depth + n, z.edge[k], stride=z.rows[k]), :]
            if n < z.rows[k]:
                first = half[pl.ds(z.start[k] + n, z.edge[k], stride=z.rows[k]), :]
            put_edges(pair, other, (pl.ds(n * z.rims + z.rim[k], z.edge[k]), everything), last, first)


def inside(z, depth, above):
    at = lax.axis_index("row")
    large = lax.broadcasted_iota(jnp.int32, (z.rims, 1), 0) < z.rim[0]
    parts = []
    for n in range(depth):
        if above:
            ok = [jnp.where(at * rows >= depth - n, 1.0, 0.0) for rows in z.rows]
        else:
            ok = [jnp.where((at + 1) * rows + n + 1 <= height, 1.0, 0.0) for rows, height in zip(z.rows, HEIGHTS)]
        parts.append(jnp.where(large, ok[1], ok[0]).astype(F32))
    return jnp.concatenate(parts, axis=0)


def clear_guards(z, pads, a):
    for k in (0, 1):
        pads[k][a, 1, pl.ds(0, z.step[k]), :] = jnp.zeros((z.step[k], 128), F32)
        pads[k][a, 0, pl.ds(z.step[k] + z.count[k], z.step[k]), :] = jnp.zeros((z.step[k], 128), F32)


def fill_center(z, pads, value):
    clear_guards(z, pads, 1)
    for k in (0, 1):
        for h in (0, 1):
            pads[k][1, h, pl.ds(z.step[k], z.count[k]), :] = value[z.start[k] : z.start[k] + z.count[k], 128 * h : 128 * h + 128]


def fill_shifted(z, pads, above, below):
    for k in (0, 1):
        ref, step, count, rows = pads[k], z.step[k], z.count[k], z.rows[k]
        rim = slice(z.rim[k], z.rim[k] + z.edge[k])
        for h in (0, 1):
            lanes = slice(128 * h, 128 * h + 128)
            ref[0, h, pl.ds(step, count), :] = ref[1, h, pl.ds(step - 1, count), :]
            ref[2, h, pl.ds(step, count), :] = ref[1, h, pl.ds(step + 1, count), :]
            ref[0, h, pl.ds(step, z.edge[k], stride=rows), :] = above[rim, lanes]
            ref[2, h, pl.ds(step + rows - 1, z.edge[k], stride=rows), :] = below[rim, lanes]


def fill_pads(z, pads, value, above, below):
    fill_center(z, pads, value)
    fill_shifted(z, pads, above, below)
    for a in (0, 2):
        clear_guards(z, pads, a)


def beside(left, right):
    lane = lax.broadcasted_iota(jnp.int32, (1, 128), 1)
    middle = pltpu.roll(jnp.where(lane >= 64, left[1], right[1]), 64, 1)
    return [
        jnp.where(lane >= 96, left[0], jnp.where(lane < 32, right[0], middle)),
        jnp.where(lane >= 96, left[2], jnp.where(lane < 32, right[2], 0.0)),
    ]


def band_operand(z, pads):
    parts = ([], [])
    for k in (1, 0):
        ref, step, count = pads[k], z.step[k], z.count[k]
        low, high = ([ref[a, h, pl.ds(step, count), :] for a in range(TAPS)] for h in (0, 1))
        before = [ref[a, 1, pl.ds(0, count), :] for a in range(TAPS)]
        after = [ref[a, 0, pl.ds(2 * step, count), :] for a in range(TAPS)]
        parts[0].append(jnp.concatenate(low + beside(before, high), axis=1))
        parts[1].append(jnp.concatenate(high + beside(low, after), axis=1))
    return [jnp.concatenate(part, axis=0) for part in parts]


def rim_operand(z, chain, depth):
    m = lax.broadcasted_iota(jnp.int32, (z.rims, 1), 0)
    large = m < z.rim[0]
    has_before = jnp.where(large, m, m - z.rim[0]) >= jnp.where(large, z.images[1], z.images[0])
    has_after = m < jnp.where(large, z.rim[0] - z.images[1], z.rims - z.images[0])
    low, high, before, after = [], [], [], []
    for r in range(depth + 1):
        at = z.guard + r * z.rims
        low.append(chain[0, pl.ds(at, z.rims), :])
        high.append(chain[1, pl.ds(at, z.rims), :])
        shifted = [chain[1, pl.ds(at - images, z.rims), :] for images in z.images]
        before.append(jnp.where(has_before, jnp.where(large, shifted[1], shifted[0]), 0.0))
        shifted = [chain[0, pl.ds(at + images, z.rims), :] for images in z.images]
        after.append(jnp.where(has_after, jnp.where(large, shifted[1], shifted[0]), 0.0))
    parts = ([], [])
    for n in range(depth - 1):
        rows = slice(n, n + TAPS)
        parts[0].append(jnp.concatenate(low[rows] + beside(before[rows], high[rows]), axis=1))
        parts[1].append(jnp.concatenate(high[rows] + beside(low[rows], after[rows]), axis=1))
    return [jnp.concatenate(part, axis=0) for part in parts]


def times(parts, weight):
    left = jnp.concatenate([part[h] for h in (0, 1) for part in parts], axis=0)
    both = jnp.concatenate([weight_matrix(weight.at[0]), weight_matrix(weight.at[1])], axis=1)
    result = dot(jnp.concatenate(split(left), axis=1), jnp.concatenate([both, both], axis=0))
    result = result[:, :128] + result[:, 128:]
    rows = result.shape[0] // 2
    return jnp.concatenate([result[:rows], result[rows:]], axis=1)


def rim_operands(z, pads, above, below, depth, chains):
    parts = []
    for side, (rim, chain) in enumerate(zip((above, below), chains)):
        rim_at, own_at = (z.guard, z.guard + depth * z.rims) if side == 0 else (z.guard + z.rims, z.guard)
        for h in (0, 1):
            chain[h, pl.ds(rim_at, depth * z.rims), :] = rim[:, 128 * h : 128 * h + 128]
            for k in (0, 1):
                row = z.step[k] + (0 if side == 0 else z.rows[k] - 1)
                chain[h, pl.ds(own_at + z.rim[k], z.edge[k]), :] = pads[k][1, h, pl.ds(row, z.edge[k], stride=z.rows[k]), :]
        parts.append(rim_operand(z, chain, depth))
    return parts


def convolve(z, own, above, below, depth, pads, chains, weight):
    r = z.rims
    fill_pads(z, pads, own, above[(depth - 1) * r :], below[:r])
    parts = [band_operand(z, pads)]
    if depth > 1:
        parts += rim_operands(z, pads, above, below, depth, chains)
    result = times(parts, weight)
    n = z.total + (depth - 1) * r
    return result[: z.total], result[z.total : n], result[n:]


def convolve_rims(z, pads, above, below, depth, chains, weight):
    result = times(rim_operands(z, pads, above, below, depth, chains), weight)
    n = (depth - 1) * z.rims
    return result[:n], result[n:]


def image_sums(z, value):
    slot = lax.broadcasted_iota(jnp.int32, (z.slots, 1), 0)
    sums = jnp.zeros((z.slots, 128), F32)
    for k in (0, 1):
        line = value[z.start[k] : z.start[k] + z.step[k]]
        for j in range(1, z.blocks[k]):
            at = z.start[k] + j * z.step[k]
            line = line + value[at : at + z.step[k]]
        image = lax.broadcasted_iota(jnp.int32, (z.step[k], 1), 0) // z.rows[k]
        for i in range(z.images[k]):
            sums = jnp.where(slot == i + k * z.images[0], column_sum(jnp.where(image == i, line, 0.0)), sums)
    return sums


def image_rows(z, values, rims):
    parts = []
    for k in (1, 0):
        image = lax.broadcasted_iota(jnp.int32, (z.step[k], 1), 0) // z.rows[k]
        line = jnp.zeros((z.step[k], 128), F32)
        for i in range(z.images[k]):
            at = i + k * z.images[0]
            line = jnp.where(image == i, values[at : at + 1], line)
        parts += [line] * z.blocks[k]
    if rims:
        m = lax.broadcasted_iota(jnp.int32, (z.rims, 1), 0)
        image = jnp.where(m < z.rim[0], z.images[0] + m % z.images[1], (m - z.rim[0]) % z.images[0])
        line = jnp.zeros((z.rims, 128), F32)
        for at in range(sum(z.images)):
            line = jnp.where(image == at, values[at : at + 1], line)
        parts += [line] * rims
    return jnp.concatenate(parts, axis=0)


def channel_mean():
    a = lax.broadcasted_iota(jnp.int32, (LANES, 128), 0) // C
    b = lax.broadcasted_iota(jnp.int32, (LANES, 128), 1) % 64
    return jnp.where(a == b, 1.0 / C, 0.0).astype(F32)


def to_channels():
    a = lax.broadcasted_iota(jnp.int32, (128, LANES), 0)
    b = lax.broadcasted_iota(jnp.int32, (128, LANES), 1) // C
    return jnp.where(a == b, 1.0, 0.0).astype(F32)


def attention(value):
    return spread(value * value, channel_mean())


def pieces(source, target):
    return [(source.at[n], target.at[n]) for n in range(source.shape[0])]


def copies_of(pairs, sems, first=0):
    return [pltpu.make_async_copy(a, b, sems.at[first + n]) for n, (a, b) in enumerate(pairs)]


def start_all(copies):
    for copy in copies:
        copy.start()


def wait_all(copies):
    for copy in copies:
        copy.wait()


def start_kernel(z, small, large, up_s, up_l, t_s, t_l, x, pair, other, copies, raw, half, sems):
    images = [(small, raw[0])] + pieces(large, raw[1])
    rest = [(up_s, raw[2])] + pieces(up_l, raw[3]) + [(t_s, raw[4]), (t_l, raw[5])]
    loads = copies_of(images + rest, sems)
    start_all(loads)
    r, n = z.rims, REACH * z.rims
    tail = n + 2 * r
    for ref in (pair, other):
        ref[pl.ds(tail, z.slots), :] = jnp.zeros((z.slots, LANES), F32)
    wait_all(loads[: len(images)])
    to_matrix(z, raw[:2], half)
    value = whole(half)
    x[...] = value
    moments(z, value, copies)
    for h in (0, 1):
        lanes = pl.ds(128 * h, 128)
        take_rims(z, half.at[h], REACH, pair.at[pl.ds(0, n), lanes], other.at[pl.ds(0, n), lanes])
    wait_all(loads[len(images) :])
    for k in (0, 1):
        width, rows = HEIGHTS[k], z.rows[k]
        for i in range(z.images[k]):
            slot = pl.ds(tail + i + k * z.images[0], 1)
            for d in (0, 1):
                has_last, has_first = rows + d >= 2, d < rows
                last, first = pl.ds(max(rows - 2 + d, 0), 1), pl.ds(min(d, rows - 1), 1)
                for j in range(z.blocks[k]):
                    lanes = pl.ds(LANES * j, LANES)
                    at = (pl.ds(n + d * r + z.rim[k] + j * z.images[k] + i, 1), pl.ds(0, LANES))
                    nothing = jnp.zeros((1, LANES), F32)
                    put_edges(
                        pair, other, at,
                        raw[2 + k][i, last, lanes] if has_last else nothing,
                        raw[2 + k][i, first, lanes] if has_first else nothing,
                    )
                nothing = jnp.zeros((1, width), F32)
                put_edges(
                    pair, other, (slot, pl.ds(128 * d, width)),
                    raw[4 + k][i, last, :] if has_last else nothing,
                    raw[4 + k][i, first, :] if has_first else nothing,
                )


def banded(taps, ref):
    row = lax.broadcasted_iota(jnp.int32, (128, 128), 0) // C
    lane = group_of(128)
    for a in range(TAPS):
        main = jnp.zeros((128, 128), F32)
        for b in range(TAPS):
            main = jnp.where(row - lane + 1 == b, taps[a][b], main)
        before = jnp.where(lane[:C] == 0, taps[a][0][:C], 0.0)
        after = jnp.where(lane[:C] == 3, taps[a][2][:C], 0.0)
        for n, part in enumerate(split(jnp.concatenate([main, before, after], axis=0))):
            ref[n, pl.ds(a * TAP_ROWS, TAP_ROWS), :] = part


def weight_matrix(ref):
    main = [ref[pl.ds(a * TAP_ROWS, 128), :] for a in range(TAPS)]
    before, after = ([ref[pl.ds(a * TAP_ROWS + 128 + n * C, C), :] for a in range(TAPS)] for n in (0, 1))
    return jnp.concatenate(
        main + [after[0], before[1], after[1], before[0], after[2], jnp.zeros((2 * C, 128), BF16), before[2]], axis=0
    )


def prepare_kernel(z, first, second, up_s, up_l, t_s, t_l, g1, b1, g2, b2, x, w1, w2, weights, affine, upstream, teacher, x_copy, raw, kept, kept_u, rows, half, sems):
    targets = tuple(raw) + tuple(rows.at[pl.ds(n, 1), :] for n in range(4))
    refs = (first, second, up_s, up_l, t_s, t_l, g1, b1, g2, b2)
    loads = [pltpu.make_async_copy(a, b, sems.at[n]) for n, (a, b) in enumerate(zip(refs, targets))]
    start_all(loads)
    stores = [pltpu.make_async_copy(x, x_copy, sems.at[13])]
    stores[0].start()
    wait_all(loads)
    to_matrix(z, raw[2:4], half)
    kept_u[...] = whole(half)
    stores.append(pltpu.make_async_copy(kept_u, upstream, sems.at[10]))
    stores[1].start()
    for n, (source, forward) in enumerate(zip(raw[:2], (w1, w2))):
        tiles = []
        for a in range(TAPS):
            line = [jnp.concatenate([source[a, b]] * 4, axis=1) for b in range(TAPS)]
            tiles.append([jnp.concatenate([tap] * 4, axis=0) for tap in line])
        turned = [[tiles[TAPS - 1 - a][TAPS - 1 - b].T for b in range(TAPS)] for a in range(TAPS)]
        banded(tiles, forward)
        if n == 0:
            stores.append(pltpu.make_async_copy(forward, weights.at[2], sems.at[14]))
            stores[-1].start()
        banded(turned, kept.at[n])
        stores.append(pltpu.make_async_copy(kept.at[n], weights.at[n], sems.at[11 + n]))
        stores[-1].start()
    taps = sum(raw[0][a, b] for a in range(TAPS) for b in range(TAPS))
    pivot = dot(jnp.broadcast_to(gelu(rows[1:2]), (8, C)), taps)[0:1]
    affine[...] = jnp.concatenate([jnp.concatenate([rows[...], pivot], axis=0)] * BLOCK, axis=1)
    teacher[...] = jnp.zeros(teacher.shape, F32)
    for k, ref in ((0, raw[4]), (1, raw[5])):
        for i in range(z.images[k]):
            line = ref[i]
            for j in range(z.blocks[k]):
                at = z.start[k] + j * z.step[k] + i * z.rows[k]
                for lane in (0, 64):
                    teacher[pl.ds(at, z.rows[k]), pl.ds(lane, BLOCK)] = line[:, j * BLOCK : (j + 1) * BLOCK]
    wait_all(stores)


def normed_by(stats):
    return lambda v: (v - stats[0:1]) * stats[1:2]


def activation(center, scale, gain, bias):
    factor = scale * gain
    offset = bias - center * factor
    return lambda v: gelu(v * factor + offset)


def first_kernel(z, x, pair, other, gathered, affine, weight, hidden, stats, copies, pads):
    center, scale = merged(z, gathered)
    act = activation(center, scale, affine[0:1], affine[1:2])
    r, lanes = z.rims, pl.ds(0, LANES)
    up = act(above_of(pair, other, (pl.ds((REACH - 1) * r, r), lanes))) * inside(z, 1, True)
    down = act(below_of(pair, other, (pl.ds(0, r), lanes))) * inside(z, 1, False)
    own, _, _ = convolve(z, act(x[...]), up, down, 1, pads, None, weight)
    moments(z, own, copies)
    hidden[...] = own
    stats[0:1] = center
    stats[1:2] = scale


def second_kernel(z, hidden, h_above, h_below, gathered, affine, weight, x, pair, other, teacher, out, o_above, o_below, near, stats, copies, pads, chains):
    center, scale = merged(z, gathered)
    act = activation(center, scale, affine[2:3], affine[3:4])
    r = z.rims
    own = act(hidden[...])
    up, down = act(h_above[...]) * inside(z, 3, True), act(h_below[...]) * inside(z, 3, False)
    own, up, down = convolve(z, own, up, down, 3, pads, chains, weight)
    own = x[...] + own
    amap = attention(own)
    lane = lax.broadcasted_iota(jnp.int32, (1, 128), 1)
    sums = image_sums(z, amap * jnp.where(lane < 64, amap, teacher[...]))
    copies[...] = jnp.concatenate([sums] * z.peers, axis=0)
    out[...] = own
    o_above[...] = above_of(pair, other, (pl.ds(2 * r, 2 * r), pl.ds(0, LANES))) + up
    o_below[...] = below_of(pair, other, (pl.ds(0, 2 * r), pl.ds(0, LANES))) + down
    near[0] = h_above[pl.ds(2 * r, r), :]
    near[1] = h_below[pl.ds(0, r), :]
    stats[0:1] = center
    stats[1:2] = scale


def tap_rows(q):
    return 128 + C if q < 0 else q * C


def tap_product(z, operand, own, above, below, pads):
    fill_center(z, pads, own)
    fill_shifted(z, pads, above, below)
    columns = []
    for a in range(TAPS):
        columns.append(
            jnp.concatenate([pads[k][TAPS - 1 - a, h, pl.ds(z.step[k], z.count[k]), :] for h in (0, 1) for k in (1, 0)], axis=0)
        )
    used = [jnp.concatenate([operand[n, pl.ds(0, 128 + C), :], operand[n, pl.ds(256 - C, C), :]], axis=0) for n in (0, 1)]
    return product(used, split(jnp.concatenate(columns, axis=1)))


def tap_sums(result, tiles, first_group):
    group = group_of()
    for a in range(TAPS):
        for b in range(TAPS):
            total = None
            for p in range(4):
                at = tap_rows(p + b - 1)
                part = result[at : at + C, 128 * a : 128 * a + 128]
                total = part if total is None else jnp.where(group == p, part, total)
            tile, slot = divmod(first_group + a * TAPS + b, 4)
            tiles[tile] = jnp.where(group == slot, spread_groups(total), tiles[tile])


def tap_counts(z, turned, tiles, first_group):
    group = group_of()
    m = lax.broadcasted_iota(jnp.int32, (1, 2 * z.total), 1) % z.total
    row = jnp.where(m < z.start[0], m % z.rows[1], (m - z.start[0]) % z.rows[0])
    height = jnp.where(m < z.start[0], z.rows[1], z.rows[0])
    at = lax.axis_index("row")
    lost = {
        0: (row == height - 1) & (at == z.peers - 1),
        2: (row == 0) & (at == 0),
    }
    for a in range(TAPS):
        column = jnp.sum(jnp.where(lost[a], 0.0, turned) if a in lost else turned, axis=1, keepdims=True)
        used = jnp.concatenate([column[: 128 + C], column[256 - C :]], axis=0)
        for b in range(TAPS):
            total = sum(used[tap_rows(p + b - 1) : tap_rows(p + b - 1) + C] for p in range(4))
            tile, slot = divmod(first_group + a * TAPS + b, 4)
            tiles[tile] = jnp.where(group == slot, total, tiles[tile])


def turned_operand(z, value, pads, kept):
    fill_center(z, pads, value)
    lane = lax.broadcasted_iota(jnp.int32, (1, 128), 1)
    halves = ([], [])
    for k in (1, 0):
        ref, step, count = pads[k], z.step[k], z.count[k]
        low, high = ref[1, 0, pl.ds(step, count), :], ref[1, 1, pl.ds(step, count), :]
        before, after = ref[1, 1, pl.ds(0, count), :], ref[1, 0, pl.ds(2 * step, count), :]
        for part, main, left, right in ((halves[0], low, before, high), (halves[1], high, low, after)):
            part.append(jnp.concatenate([main, jnp.where(lane >= 96, left, jnp.where(lane < 32, right, 0.0))], axis=1))
    turned = jnp.concatenate(halves[0] + halves[1], axis=0).T
    parts = split(turned)
    for n in (0, 1):
        kept[n] = parts[n]
    return turned


def first_operand_kernel(z, x, hidden, pair, other, stats, affine, teacher, upstream, weights, h_above, h_below, left, packed, teachers, spread_u, near_u, pads, chains, deep_chains, kept, kept_w, kept_u, pixels, kept_t, kept_c, kept_packed, sems):
    r, own = z.rims, pl.ds(0, z.total)
    loads = copies_of([(upstream, kept_u.at[own, :]), (weights.at[1], kept_w.at[1])], sems)
    first = pltpu.make_async_copy(weights.at[2], kept_w.at[0], sems.at[7])
    first.start()
    start_all(loads)
    act = activation(stats[0:1], stats[1:2], affine[0:1], affine[1:2])
    value = turned_operand(z, act(x[...]), pads, kept)
    stores = [pltpu.make_async_copy(kept, left, sems.at[2])]
    stores[0].start()
    n, lanes = REACH * r, pl.ds(0, LANES)
    up = act(above_of(pair, other, (pl.ds(0, n), lanes))) * inside(z, REACH, True)
    down = act(below_of(pair, other, (pl.ds(0, n), lanes))) * inside(z, REACH, False)
    first.wait()
    up, down = convolve_rims(z, pads, up, down, REACH, deep_chains, kept_w.at[0])
    h_above[...] = up
    h_below[...] = down
    tiles = [jnp.zeros((C, 128), F32) for _ in range(BACK_LANES // 128)]
    tap_counts(z, value, tiles, ONES)
    pivot = affine[4:5]
    result = tap_product(
        z, kept, hidden[...] - pivot, (up[2 * r :] - pivot) * inside(z, 1, True),
        (down[:r] - pivot) * inside(z, 1, False), pads,
    )
    tap_sums(result, tiles, HIDDEN)
    kept_packed[...] = jnp.concatenate(tiles, axis=1)
    stores.append(pltpu.make_async_copy(kept_packed, packed, sems.at[6]))
    stores[1].start()
    pixels[own, :] = teacher[...]
    pixels[pl.ds(z.total, 4 * r), :] = jnp.zeros((4 * r, 128), F32)
    n = (REACH + 2) * r
    for side, beyond_of in enumerate((above_of, below_of)):
        for d in (0, 1):
            for k in (0, 1):
                line = beyond_of(pair, other, (pl.ds(n + k * z.images[0], z.images[k]), pl.ds(128 * d, 128)))
                for j in range(z.blocks[k]):
                    at = z.total + (2 * side + d) * r + z.rim[k] + j * z.images[k]
                    pixels[pl.ds(at, z.images[k]), pl.ds(0, BLOCK)] = line[:, j * BLOCK : (j + 1) * BLOCK]
    kept_t[...] = spread(pixels[...], to_channels())
    stores.append(pltpu.make_async_copy(kept_t, teachers, sems.at[3]))
    stores[2].start()
    n = REACH * r
    at = (pl.ds(n, 2 * r), pl.ds(0, LANES))
    up, down = above_of(pair, other, at) * inside(z, 2, True), below_of(pair, other, at) * inside(z, 2, False)
    kept_u[pl.ds(z.total, r), :] = up[r:]
    kept_u[pl.ds(z.total + r, r), :] = down[:r]
    wait_all(loads)
    stores.append(pltpu.make_async_copy(kept_u, near_u, sems.at[5]))
    stores[3].start()
    kept_c[...] = jnp.concatenate(convolve(z, kept_u[own, :], up, down, 2, pads, chains, kept_w.at[1]), axis=0)
    stores.append(pltpu.make_async_copy(kept_c, spread_u, sems.at[4]))
    stores[4].start()
    wait_all(stores)


def second_operand_kernel(z, hidden, near, stats, affine, out, o_above, o_below, teachers, spread_u, near_u, weights, out_copy, hidden_copy, left, shifts, by_map, by_teacher, up, pads, chains, kept_t, kept_u, kept_w, kept_s, sems):
    r, total = z.rims, z.total
    loads = [
        pltpu.make_async_copy(teachers, kept_t, sems.at[0]),
        pltpu.make_async_copy(weights.at[1], kept_w, sems.at[1]),
        pltpu.make_async_copy(spread_u, kept_u, sems.at[2]),
    ]
    start_all(loads)
    stores = [
        pltpu.make_async_copy(out, out_copy, sems.at[4]),
        pltpu.make_async_copy(hidden, hidden_copy.at[pl.ds(0, total), :], sems.at[7]),
        pltpu.make_async_copy(near.at[0], hidden_copy.at[pl.ds(total, r), :], sems.at[8]),
        pltpu.make_async_copy(near.at[1], hidden_copy.at[pl.ds(total + r, r), :], sems.at[9]),
        pltpu.make_async_copy(near_u, up, sems.at[10]),
    ]
    start_all(stores)
    normed = normed_by(stats)(jnp.concatenate([hidden[...], near[0], near[1]], axis=0))
    shifted = normed * affine[2:3] + affine[3:4]
    turned_operand(z, gelu(shifted[:total]), pads, left)
    ones = jnp.ones((total, 1), F32)
    masks = jnp.concatenate([ones, inside(z, 1, True), inside(z, 1, False)], axis=0)
    slopes = gelu_slope(shifted) * masks
    o = jnp.concatenate([out[...], o_above[...] * inside(z, 2, True), o_below[...] * inside(z, 2, False)], axis=0)
    for_map = spread(attention(o), to_channels()) * o
    wait_all(loads)
    for_teacher = kept_t[...] * o
    kept_s[0] = kept_u[...] * slopes
    stores += copies_of(pieces(kept_s, shifts), sems, 11)
    stores[-3].start()
    for n, value, ref in ((1, for_map, by_map), (2, for_teacher, by_teacher)):
        own, before, after = value[:total], value[total : total + 2 * r], value[total + 2 * r :]
        ref[...] = jnp.concatenate([own, before[r:], after[:r]], axis=0)
        kept_s[n] = jnp.concatenate(convolve(z, own, before, after, 2, pads, chains, kept_w), axis=0) * slopes
        stores[n - 3].start()
    wait_all(stores)


def upstream_kernel(z, gathered, up, shifts, left_1, left_2, packed, by_map, by_teacher, hidden, stats, dout, dshift, d_above, d_below, slabs, kept_s, kept_left, kept_h, kept_packed, pads, more_pads, sems):
    r, total = z.rims, z.total
    loads = copies_of(
        pieces(shifts, kept_s) + pieces(left_1, kept_left) + [(hidden.at[pl.ds(0, total), :], kept_h), (packed, kept_packed)], sems
    )
    start_all(loads)
    lane = lax.broadcasted_iota(jnp.int32, (z.slots, 128), 1)
    sums = sum(gathered[pl.ds(n * z.slots, z.slots), :] for n in range(z.peers))
    square = jnp.sum(jnp.where(lane < 64, sums, 0.0), axis=1, keepdims=True)
    cross = jnp.sum(jnp.where(lane < 64, 0.0, sums), axis=1, keepdims=True)
    inverse = lax.rsqrt(square + map_eps)
    inner = beta_weight * (square * inverse - cross) * inverse
    shape = (z.slots, 128)
    for_map = (beta_weight - inner) * inverse * inverse * (2.0 / C)
    for_teacher = beta_weight * inverse * (2.0 / C)
    for_map, for_teacher = (wide(image_rows(z, jnp.broadcast_to(v, shape), 2)) for v in (for_map, for_teacher))
    value = up[...] + for_map * by_map[...] - for_teacher * by_teacher[...]
    dout[...] = value[:total]
    second = tap_product(z, left_2, value[:total], value[total : total + r], value[total + r :], pads)
    wait_all(loads[:3])
    shift = kept_s[0] + for_map * kept_s[1] - for_teacher * kept_s[2]
    pre, above, below = shift[:total], shift[total : total + r], shift[total + r :]
    dshift[...] = pre
    d_above[...] = above
    d_below[...] = below
    wait_all(loads[3:5])
    first = tap_product(z, kept_left, pre, above, below, more_pads)
    wait_all(loads[5:])
    normed = normed_by(stats)(kept_h[...])
    tiles = [kept_packed[:, 128 * n : 128 * n + 128] for n in range(BACK_LANES // 128)]
    group = group_of()
    tiles[0] = jnp.where(group == BIAS, fold(column_sum(pre)), jnp.where(group == GAIN, fold(column_sum(pre * normed)), tiles[0]))
    tap_sums(second, tiles, SECOND)
    tap_sums(first, tiles, LEFT)
    line = jnp.concatenate(tiles, axis=1)
    for d in range(z.devices):
        slabs[d] = line[d % C : d % C + 1]


def write_kernel(z, out, x, hidden, weights, first_stats, stats, order, out_s, out_l, first_normed, normed, weight, kept, kept_x, kept_h, half, sems):
    loads = [pltpu.make_async_copy(a, b, sems.at[n]) for n, (a, b) in enumerate(((out, kept), (x, kept_x), (hidden, kept_h), (weights.at[0], weight)))]
    start_all(loads)
    loads[0].wait()
    put_halves(half, kept[...])
    from_matrix(z, half, (out_s, out_l))
    loads[1].wait()
    first_normed[...] = normed_by(first_stats)(kept_x[...])
    loads[2].wait()
    normed[...] = normed_by(stats)(kept_h[...])
    loads[3].wait()


def norm_sums(total):
    group = group_of()
    return [wide(spread_groups(jnp.where(group == n, total[:, :128], 0.0))) for n in (BIAS, GAIN)]


def hidden_kernel(z, gathered, dshift, d_above, d_below, second_normed, stats, affine, weight, first_normed, pre_ref, norm_grads, slabs, pads):
    total = jnp.sum(gathered[...], axis=0)
    bias_sum, gain_sum = norm_sums(total)
    norm_grads[0:1] = bias_sum[:, :128]
    norm_grads[1:2] = gain_sum[:, :128]
    bias_mean, gain_mean = bias_sum / z.pixels, gain_sum / z.pixels
    factor = affine[2:3] * stats[1:2]
    r, total_rows = z.rims, z.total

    def back(d, normed):
        return factor * (d - bias_mean - normed * gain_mean)

    own = back(dshift[...], second_normed[pl.ds(0, total_rows), :])
    up = back(d_above[...], second_normed[pl.ds(total_rows, r), :]) * inside(z, 1, True)
    down = back(d_below[...], second_normed[pl.ds(total_rows + r, r), :]) * inside(z, 1, False)
    grad, _, _ = convolve(z, own, up, down, 1, pads, None, weight)
    normed = first_normed[...]
    pre = grad * gelu_slope(normed * affine[0:1] + affine[1:2])
    pre_ref[...] = pre
    lane = lax.broadcasted_iota(jnp.int32, (1, 128), 1)
    taps = TAPS * TAPS * C

    def along(row):
        return jnp.concatenate([row[:, :128]] * 3, axis=1)[:, :taps]

    second, left, against, ones = (total[:, n * C : n * C + taps] for n in (SECOND, LEFT, HIDDEN, ONES))
    against = along(stats[1:2]) * (against - along(stats[0:1] - affine[4:5]) * ones)
    first = along(factor) * (left - along(bias_mean) * ones - along(gain_mean) * against)
    sums = jnp.where(lane < C, fold(column_sum(pre)), fold(column_sum(pre * normed)))
    line = jnp.concatenate([sums[:, : 2 * C], second, first], axis=1)
    slabs[...] = jnp.broadcast_to(line[None], slabs.shape)


def back_kernel(z, gathered, pre, normed, stats, affine, dout, second_grads, back_s, back_l, one, two, gain_out, bias_out, second_gain, second_bias, half, lines):
    bias_sum, gain_sum = norm_sums(jnp.sum(gathered[:, :, pl.ds(0, 128)], axis=0))
    bias_out[...] = bias_sum[:, :C]
    gain_out[...] = gain_sum[:, :C]
    second_bias[...] = second_grads[0:1, pl.ds(0, C)]
    second_gain[...] = second_grads[1:2, pl.ds(0, C)]
    value = dout[...] + affine[0:1] * stats[1:2] * (pre[...] - bias_sum / z.pixels - normed[...] * (gain_sum / z.pixels))
    put_halves(half, value)
    from_matrix(z, half, (back_s, back_l))
    for d in range(C):
        lines[pl.ds(d, 1), :] = gathered[d]
    for ref, group in ((two, LAST_SECOND), (one, LAST_FIRST)):
        for a in range(TAPS):
            for b in range(TAPS):
                at = (group + a * TAPS + b) * C
                ref[a, b] = lines[:, pl.ds(at, C)]


def call(body, ins, outs, scratch=(), sems=0):
    space = {"v": pltpu.VMEM, "h": pltpu.HBM, "V": pltpu.VMEM}
    shapes = []
    for item in scratch:
        if isinstance(item, list):
            shapes.append([pltpu.VMEM(*s) for s in item])
        else:
            shapes.append(pltpu.VMEM(*item))
    if sems:
        shapes.append(pltpu.SemaphoreType.DMA((sems,)))
    run = pl.pallas_call(
        body,
        out_shape=[jax.ShapeDtypeStruct(shape, kind) if s == "v" else space[s](shape, kind) for s, shape, kind in outs],
        in_specs=[pl.BlockSpec(memory_space=space[s]) for s in ins],
        out_specs=[pl.BlockSpec(memory_space=space[s]) for s, _, _ in outs],
        scratch_shapes=shapes,
        compiler_params=pltpu.CompilerParams(vmem_limit_bytes=VMEM_LIMIT),
    )
    return lambda *args: run(
        *(pltpu.with_memory_space_constraint(arg, pltpu.HBM) if s == "h" else arg for s, arg in zip(ins, args))
    )


def exchange(lines, axes):
    shape = lines.shape
    if len(shape) == 2:
        lines = lines.reshape(math.prod(lax.axis_size(axis) for axis in axes), -1, 128)
    return lax.all_to_all(lines, axes, 0, 0, tiled=True).reshape(shape)


def beyond(z, pair, other, depths):
    hops = max(-(-depth // rows) for rows in z.rows for depth in depths)
    if hops == 1:
        swap = lambda value, start: lax.ppermute(
            value, "row", [(i + a, i + 1 - a) for i in range(start, z.peers - 1, 2) for a in (0, 1)]
        )
        others = swap(other, 1)
        return swap(pair, 0), others
    even = is_even()
    bottom, top = jnp.where(even, pair, other), jnp.where(even, other, pair)
    above, below = [], []
    for hop in range(1, hops + 1):
        above.append(lax.ppermute(bottom, "row", [(i, i + hop) for i in range(z.peers - hop)]))
        below.append(lax.ppermute(top, "row", [(i + hop, i) for i in range(z.peers - hop)]))
    up, down = [], []
    base = 0
    for depth in depths:
        for n in range(depth):
            for k in (1, 0):
                hop, back = divmod(depth - 1 - n, z.rows[k])
                at = base + (depth - 1 - back) * z.rims + z.rim[k]
                up.append(above[hop][at : at + z.edge[k]])
                hop, back = divmod(n, z.rows[k])
                at = base + back * z.rims + z.rim[k]
                down.append(below[hop][at : at + z.edge[k]])
        base += depth * z.rims
    up.append(jnp.concatenate([pixel_rows(z, above, base, 1, 1), pixel_rows(z, above, base, 0, 1)], axis=1))
    down.append(jnp.concatenate([pixel_rows(z, below, base, 0, 0), pixel_rows(z, below, base, 1, 0)], axis=1))
    up, down = jnp.concatenate(up, axis=0), jnp.concatenate(down, axis=0)
    return jnp.where(even, down, up), jnp.where(even, up, down)


def pixel_rows(z, bands, base, distance, last):
    lines = []
    for k in (0, 1):
        hop, back = divmod(distance, z.rows[k])
        at = base + k * z.images[0]
        half = 128 * abs(last - back)
        lines.append(bands[hop][at : at + z.images[k], half : half + 128])
    lines.append(jnp.zeros((z.slots - sum(z.images), 128), F32))
    return jnp.concatenate(lines, axis=0)


def local(
    image_small, image_large, teacher_small, teacher_large, upstream_small, upstream_large,
    conv_first, gain_first, bias_first, conv_second, gain_second, bias_second,
):
    peers = lax.axis_size("row")
    devices = lax.axis_size("img") * peers
    z = Sizes(image_small.shape, image_large.shape, devices, peers)
    body = lambda function: functools.partial(function, z)
    r = z.rims
    full, half, pair = (z.total, LANES), (2, z.total, 128), (2 * devices, 128)
    weight, left = (2, TAPS * TAP_ROWS, 128), (2, 256, 2 * z.total)
    images = [image_small, image_large, upstream_small, upstream_large, teacher_small, teacher_large]
    f = lambda space, *shape: (space, shape, F32)
    depths = (REACH, 2)
    rim_rows = sum(depths) * r + z.slots

    x, pair_edge, other_edge, copies = call(
        body(start_kernel),
        "hhhhhh",
        [("v", full, F32), f("v", rim_rows, LANES), f("v", rim_rows, LANES), ("V", pair, F32)],
        [[(a.shape, F32) for a in images], (half, F32)],
        4 + 2 * z.images[1],
    )(*images)
    gathered = exchange(copies, AXES)
    pair_rims, other_rims = beyond(z, pair_edge, other_edge, depths)
    params = [conv_first, conv_second] + images[2:]
    w1, w2, weights, affine, upstream, teacher, x_copy = call(
        body(prepare_kernel),
        "hhhhhhhhhhv",
        [("v", weight, BF16), ("v", weight, BF16), ("h", (3,) + weight, BF16), f("v", 5, LANES), ("h", full, F32), f("v", z.total, 128), ("h", full, F32)],
        [[(a.shape, F32) for a in params], ((2,) + weight, BF16), (full, F32), ((4, C), F32), (half, F32)],
        15,
    )(*params, *(v.reshape(1, C) for v in (gain_first, bias_first, gain_second, bias_second)), x)

    hidden, stats_one, copies = call(
        body(first_kernel),
        "vvvvvv",
        [("v", full, F32), f("v", 2, LANES), ("V", pair, F32)],
        [z.pads()],
    )(x, pair_rims, other_rims, gathered, affine, w1)
    gathered = exchange(copies, AXES)
    extended, near_rows = z.total + 4 * r, z.total + 2 * r
    h_above, h_below, left_one, packed, teachers, spread_u, near_u = call(
        body(first_operand_kernel),
        "vvvvvvvhh",
        [f("v", 3 * r, LANES), f("v", 3 * r, LANES), ("h", left, BF16), f("h", C, BACK_LANES), f("h", extended, LANES), f("h", near_rows, LANES), f("h", near_rows, LANES)],
        [
            z.pads(), z.chains(2), z.chains(REACH), (left, BF16), ((2,) + weight, BF16), ((near_rows, LANES), F32), ((extended, 128), F32),
            ((extended, LANES), F32), ((near_rows, LANES), F32), ((C, BACK_LANES), F32),
        ],
        8,
    )(x, hidden, pair_rims, other_rims, stats_one, affine, teacher, upstream, weights)
    gathered, near_u = lax.optimization_barrier((gathered, near_u))

    map_shape = (peers * z.slots, 128)
    out, o_above, o_below, near, stats_two, copies = call(
        body(second_kernel),
        "vvvvvvvvvv",
        [("v", full, F32), f("v", 2 * r, LANES), f("v", 2 * r, LANES), f("v", 2, r, LANES), f("v", 2, LANES), ("V", map_shape, F32)],
        [z.pads(), z.chains(3)],
    )(hidden, h_above, h_below, gathered, affine, w2, x, pair_rims, other_rims, teacher)
    gathered = exchange(copies, ("row",))
    out_copy, hidden_copy, left_two, shifts, by_map, by_teacher, up = call(
        body(second_operand_kernel),
        "vvvvvvvhhhh",
        [
            ("h", full, F32), f("h", near_rows, LANES), ("v", left, BF16), f("h", 3, near_rows, LANES),
            f("v", near_rows, LANES), f("v", near_rows, LANES), f("v", near_rows, LANES),
        ],
        [
            z.pads(), z.chains(2), ((extended, LANES), F32), ((near_rows, LANES), F32), (weight, BF16),
            ((3, near_rows, LANES), F32),
        ],
        14,
    )(hidden, near, stats_two, affine, out, o_above, o_below, teachers, spread_u, near_u, weights)

    dout, dshift, d_above, d_below, slabs = call(
        body(upstream_kernel),
        "vvhhvhvvhv",
        [("v", full, F32), ("v", full, F32), f("v", r, LANES), f("v", r, LANES), f("V", devices, 1, BACK_LANES)],
        [((3, near_rows, LANES), F32), (left, BF16), (full, F32), ((C, BACK_LANES), F32), z.pads(), z.pads()],
        7,
    )(gathered, up, shifts, left_one, left_two, packed, by_map, by_teacher, hidden_copy, stats_two)
    gathered = exchange(slabs, AXES)
    out_s, out_l, first_normed, second_normed, weight_back = call(
        body(write_kernel),
        "hhhhvvv",
        [("v", image_small.shape, F32), ("v", image_large.shape, F32), ("v", full, F32), f("v", near_rows, LANES), ("v", weight, BF16)],
        [(full, F32), (full, F32), ((near_rows, LANES), F32), (half, F32)],
        4,
    )(out_copy, x_copy, hidden_copy, weights, stats_one, stats_two, d_above)

    pre, norm_grads, slabs = call(
        body(hidden_kernel),
        "vvvvvvvvv",
        [("v", full, F32), f("v", 2, 128), f("V", devices, 1, LAST_LANES)],
        [z.pads()],
    )(gathered, dshift, d_above, d_below, second_normed, stats_two, affine, weight_back, first_normed)
    gathered = exchange(slabs, AXES)

    back_s, back_l, one, two, gain_one, bias_one, gain_two, bias_two = call(
        body(back_kernel),
        "vvvvvvv",
        [("v", a.shape, F32) for a in (image_small, image_large, conv_first, conv_second)] + [f("v", 1, C)] * 4,
        [(half, F32), ((C, LAST_LANES), F32)],
    )(gathered, pre, first_normed, stats_one, affine, dout, norm_grads)
    return (
        out_s, out_l, back_s, back_l,
        one, gain_one.reshape(C), bias_one.reshape(C),
        two, gain_two.reshape(C), bias_two.reshape(C),
    )


def solution(mesh):
    split_bands, everywhere = P("img", "row", None), P()
    return jax.shard_map(
        local,
        mesh=mesh,
        in_specs=(split_bands,) * 6 + (everywhere,) * 6,
        out_specs=(split_bands,) * 4 + (everywhere,) * 6,
        check_vma=False,
    )
```

profile of v0, /device:TPU:0, one launch (start us, length us, event | category | flops | bytes accessed | tf_op | source)
XLA Modules:
  0.0 70.4 jit_solution(11348525239940651036)
XLA Ops:
  0.6 2.0 %shard_map.195 = (f32[256,256]{1,0:T(8,128)S(1)}, f32[248,256]{1,0:T(8,128)S(1)}, f32[248,256]{1,0:T(8,128)S(1)}, f32[64,128]{1,0:T(8,128)}) custom-call(f32[4,4,1024]{2,1,0:T(4,128)} %small.1, f32[3,8,2048]{2,1,0:T(8,128)} %large.1, f32[4,4,1024]{2,1,0:T(4,128)} %up_s.3, f32[3,8,2048]{2,1,0:T(8,128)} %up_l.3, f32[4,4,32]{2,1,0:T(4,128)} %t_s.3, f32[3,8,64]{2,1,0:T(8,128)} %t_l.3), custom_call_target="tpu_custom_call" | custom-call | tf_op jit(solution)/shard_map/pallas_call | solution.py:818
  2.6 3.0 %collective-permute-start = (f32[248,256]{1,0:T(8,128)S(1)}, f32[248,256]{1,0:T(8,128)S(1)}, u32[]{:S(2)}, u32[]{:S(2)}) collective-permute-start(f32[248,256]{1,0:T(8,128)S(1)} %get-tuple-element.68), channel_id=1, source_target_pairs={{0,1},{1,0},{2,3},{3,2},{4,5},{5,4},{6,7},{7,6},{8,9},{9,8},{10,11... | collective-permute-start | bytes 761864 | tf_op jit(solution)/shard_map/ppermute | solution.py:833
  5.6 0.7 collective-permute-start.1
  6.3 7.6 %all-to-all-start = ((f32[32,2,128]{2,1,0:T(2,128)}), f32[32,2,128]{2,1,0:T(2,128)S(1)}, u32[]{:S(2)}, u32[]{:S(2)}) async-start(f32[32,2,128]{2,1,0:T(2,128)} %bitcast), calls=%async_computation | async-start | bytes 65536 | tf_op jit(solution)/shard_map/all_to_all | solution.py:827
  13.9 2.8 %shard_map.196 = (bf16[2,576,128]{2,1,0:T(8,128)(2,1)S(1)}, bf16[2,576,128]{2,1,0:T(8,128)(2,1)S(1)}, bf16[3,2,576,128]{3,2,1,0:T(8,128)(2,1)}, f32[5,256]{1,0:T...) custom-call(f32[3,3,32,32]{3,2,1,0:T(8,128)} %first.1, f32[3,3,32,32]{3,2,1,0:T(8,128)} %second.1, ...), custom_call_target="tpu_custom_call" | custom-call | tf_op jit(solution)/shard_map/pallas_call | solution.py:818
  16.8 4.3 %all-to-all-done = f32[32,2,128]{2,1,0:T(2,128)S(1)} async-done(((f32[32,2,128]{2,1,0:T(2,128)}), f32[32,2,128]{2,1,0:T(2,128)S(1)}, u32[]{:S(2)}, u32[]{:S(2)}) %all-to-all-start) | async-done | bytes 32800 | tf_op jit(solution)/shard_map/all_to_all | solution.py:827
  21.1 0.0 collective-permute-done.pair
  21.1 0.0 collective-permute-done.1.other
  21.1 1.5 %shard_map.197 = (f32[256,256]{1,0:T(8,128)S(1)}, f32[2,256]{1,0:T(2,128)S(1)}, f32[64,128]{1,0:T(8,128)}) custom-call(f32[256,256]{1,0:T(8,128)S(1)} %get-tuple-element.67.x, f32[248,256]{1,0:T(8,128)S(1)} %collective-permute-done.pair, f32[248,256]{1,0:T(8,128)S(1)} %collective-permute-done.1.other, f32[64,128]{1,0:T(8,128)S(1)} %bitcast.16, ...), custom_call_target="tpu_custom_call" | custom-call | tf_op jit(solution)/shard_map/pallas_call | solution.py:818
  22.7 2.6 %all-to-all-start.1 = ((f32[32,2,128]{2,1,0:T(2,128)}), f32[32,2,128]{2,1,0:T(2,128)S(1)}, u32[]{:S(2)}, u32[]{:S(2)}) async-start(f32[32,2,128]{2,1,0:T(2,128)} %bitcast.6), calls=%async_computation.1 | async-start | bytes 65536 | tf_op jit(solution)/shard_map/all_to_all | solution.py:827
  25.3 4.3 %shard_map.198 = (f32[120,256]{1,0:T(8,128)S(1)}, f32[120,256]{1,0:T(8,128)S(1)}, bf16[2,256,512]{2,1,0:T(8,128)(2,1)}, f32[32,1280]{1,0:T(8,128)}, f32[416,256]...) custom-call(f32[256,256]{1,0:T(8,128)S(1)} %get-tuple-element.67.x, f32[256,256]{1,0:T(8,128)S(1)} %get-tuple-element.73.hidden, ...), custom_call_target="tpu_custom_call" | custom-call | tf_op jit(solution)/shard_map/pallas_call | solution.py:818
  29.6 2.8 %all-to-all-done.1 = f32[32,2,128]{2,1,0:T(2,128)S(1)} async-done(((f32[32,2,128]{2,1,0:T(2,128)}), f32[32,2,128]{2,1,0:T(2,128)S(1)}, u32[]{:S(2)}, u32[]{:S(2)}) %all-to-all-start.1) | async-done | bytes 32800 | tf_op jit(solution)/shard_map/all_to_all | solution.py:827
  32.4 1.8 %shard_map.199 = (f32[256,256]{1,0:T(8,128)S(1)}, f32[80,256]{1,0:T(8,128)S(1)}, f32[80,256]{1,0:T(8,128)S(1)}, f32[2,40,256]{2,1,0:T(8,128)S(1)}, f32[2,256]{1,0:T(2,128)S(1)}, /*index=5*/f32[64,128]{1,0:T(8,128)}) custom-call(f32[256,256]{1,0:T(8,128)S(1)} %get-tuple-element.73.hidden, f32[120,256]{1,0:T(8,128)S(1)} %get-tuple-element.78.h_above, ...), custom_call_target="tpu_custom_call" | custom-call | tf_op jit(solution)/shard_map/pallas_call | solution.py:818
  34.2 3.3 %all-to-all-start.2 = ((f32[8,8,128]{2,1,0:T(8,128)}), f32[8,8,128]{2,1,0:T(8,128)S(1)}, u32[]{:S(2)}, u32[]{:S(2)}) async-start(f32[8,8,128]{2,1,0:T(8,128)} %bitcast.8), calls=%async_computation.2 | async-start | bytes 65536 | tf_op jit(solution)/shard_map/all_to_all | solution.py:827
  37.6 3.7 %shard_map.200 = (f32[256,256]{1,0:T(8,128)}, f32[336,256]{1,0:T(8,128)}, bf16[2,256,512]{2,1,0:T(8,128)(2,1)S(1)}, f32[3,336,256]{2,1,0:T(8,128)}, f32[336,256]...) custom-call(f32[256,256]{1,0:T(8,128)S(1)} %get-tuple-element.73.hidden, ...), custom_call_target="tpu_custom_call" | custom-call | tf_op jit(solution)/shard_map/pallas_call | solution.py:818
  41.3 2.9 %all-to-all-done.2 = f32[8,8,128]{2,1,0:T(8,128)S(1)} async-done(((f32[8,8,128]{2,1,0:T(8,128)}), f32[8,8,128]{2,1,0:T(8,128)S(1)}, u32[]{:S(2)}, u32[]{:S(2)}) %all-to-all-start.2) | async-done | bytes 32800 | tf_op jit(solution)/shard_map/all_to_all | solution.py:827
  44.2 3.3 %shard_map.201 = (f32[256,256]{1,0:T(8,128)S(1)}, f32[256,256]{1,0:T(8,128)S(1)}, f32[40,256]{1,0:T(8,128)S(1)}, f32[40,256]{1,0:T(8,128)S(1)}, f32[32,1,1280]{2,1,0:T(1,128)}) custom-call(f32[64,128]{1,0:T(8,128)S(1)} %bitcast.14, f32[336,256]{1,0:T(8,128)S(1)} %get-tuple-element.96.up, f32[3,336,256]{2,1,0:T(8,128)} %get-tuple-element.97.shifts, ...), custom_call_target="tpu_custom_call" | custom-call | tf_op jit(solution)/shard_map/pallas_call | solution.py:818
  47.5 2.8 %all-to-all-start.3 = ((f32[32,1,1280]{2,1,0:T(1,128)}), f32[32,1,1280]{2,1,0:T(1,128)S(1)}, u32[]{:S(2)}, u32[]{:S(2)}) async-start(f32[32,1,1280]{2,1,0:T(1,128)} %get-tuple-element.106), calls=%async_computation.3 | async-start | bytes 327680 | tf_op jit(solution)/shard_map/all_to_all | solution.py:827
  50.3 2.0 %shard_map.202 = (f32[4,4,1024]{2,1,0:T(4,128)}, f32[3,8,2048]{2,1,0:T(8,128)}, f32[256,256]{1,0:T(8,128)S(1)}, f32[336,256]{1,0:T(8,128)S(1)}, bf16[2,576,128]{2,1,0:T(8,128)(2,1)S(1)}) custom-call(f32[256,256]{1,0:T(8,128)} %get-tuple-element.92.out, f32[256,256]{1,0:T(8,128)} %get-tuple-element.93.x, f32[336,256]{1,0:T(8,128)} %get-tuple-element.94.hidden, ...), custom_call_target="tpu_custom_call" | custom-call | tf_op jit(solution)/shard_map/pallas_call | solution.py:818
  52.2 5.9 %all-to-all-done.3.gathered = f32[32,1,1280]{2,1,0:T(1,128)S(1)} async-done(((f32[32,1,1280]{2,1,0:T(1,128)}), f32[32,1,1280]{2,1,0:T(1,128)S(1)}, u32[]{:S(2)}, u32[]{:S(2)}) %all-to-all-start.3) | async-done | bytes 163872 | tf_op jit(solution)/shard_map/all_to_all | solution.py:827
  58.2 0.9 %shard_map.203 = (f32[256,256]{1,0:T(8,128)S(1)}, f32[2,128]{1,0:T(2,128)S(1)}, f32[32,1,640]{2,1,0:T(1,128)S(1)}) custom-call(f32[32,1,1280]{2,1,0:T(1,128)S(1)} %all-to-all-done.3.gathered, f32[256,256]{1,0:T(8,128)S(1)} %get-tuple-element.107.dshift, f32[40,256]{1,0:T(8,128)S(1)} %get-tuple-element.103.order.d_above, ...), custom_call_target="tpu_custom_call" | custom-call | tf_op jit(solution)/shard_map/pallas_call | solution.py:818
  59.1 10.2 %all_to_all.25.gathered = f32[32,1,640]{2,1,0:T(1,128)S(1)} all-to-all(f32[32,1,640]{2,1,0:T(1,128)S(1)} %get-tuple-element.112), channel_id=1, replica_groups=mesh['img'=4,'row'=8] {'img','row'}, dimensions={0} | all-to-all | bytes 163840 | tf_op jit(solution)/shard_map/all_to_all | solution.py:827
  69.4 1.0 %shard_map.204 = (f32[4,4,1024]{2,1,0:T(4,128)}, f32[3,8,2048]{2,1,0:T(8,128)}, f32[3,3,32,32]{3,2,1,0:T(8,128)}, f32[3,3,32,32]{3,2,1,0:T(8,128)}, f32[1,32]{1,...) custom-call(f32[32,1,640]{2,1,0:T(1,128)S(1)} %all_to_all.25.gathered, ...), custom_call_target="tpu_custom_call" | custom-call | tf_op jit(solution)/shard_map/pallas_call | solution.py:818
Async XLA Ops:
  2.6 18.5 %collective-permute-start = (f32[248,256]{1,0:T(8,128)S(1)}, f32[248,256]{1,0:T(8,128)S(1)}, u32[]{:S(2)}, u32[]{:S(2)}) collective-permute-start(f32[248,256]{1,0:T(8,128)S(1)} %get-tuple-element.68), channel_id=1, source_target_pairs={{0,1},{1,0},{2,3},{3,2},{4,5},{5,4},{6,7},{7,6},{8,9},{9,8},{10,11... | collective-permute-start | bytes 761864 | tf_op jit(solution)/shard_map/ppermute | solution.py:833
  5.6 15.5 %collective-permute-start.1 = (f32[248,256]{1,0:T(8,128)S(1)}, f32[248,256]{1,0:T(8,128)S(1)}, u32[]{:S(2)}, u32[]{:S(2)}) collective-permute-start(f32[248,256]{1,0:T(8,128)S(1)} %get-tuple-element.69), channel_id=1, source_target_pairs={{1,2},{2,1},{3,4},{4,3},{5,6},{6,5},{9,10},{10,9},{11,12},{12,11},... | collective-permute-start | bytes 761864 | tf_op jit(solution)/shard_map/ppermute | solution.py:833
  6.3 14.8 %all-to-all-start = ((f32[32,2,128]{2,1,0:T(2,128)}), f32[32,2,128]{2,1,0:T(2,128)S(1)}, u32[]{:S(2)}, u32[]{:S(2)}) async-start(f32[32,2,128]{2,1,0:T(2,128)} %bitcast), calls=%async_computation | async-start | bytes 65536 | tf_op jit(solution)/shard_map/all_to_all | solution.py:827
  22.7 9.8 %all-to-all-start.1 = ((f32[32,2,128]{2,1,0:T(2,128)}), f32[32,2,128]{2,1,0:T(2,128)S(1)}, u32[]{:S(2)}, u32[]{:S(2)}) async-start(f32[32,2,128]{2,1,0:T(2,128)} %bitcast.6), calls=%async_computation.1 | async-start | bytes 65536 | tf_op jit(solution)/shard_map/all_to_all | solution.py:827
  34.2 10.0 %all-to-all-start.2 = ((f32[8,8,128]{2,1,0:T(8,128)}), f32[8,8,128]{2,1,0:T(8,128)S(1)}, u32[]{:S(2)}, u32[]{:S(2)}) async-start(f32[8,8,128]{2,1,0:T(8,128)} %bitcast.8), calls=%async_computation.2 | async-start | bytes 65536 | tf_op jit(solution)/shard_map/all_to_all | solution.py:827
  47.5 10.7 %all-to-all-start.3 = ((f32[32,1,1280]{2,1,0:T(1,128)}), f32[32,1,1280]{2,1,0:T(1,128)S(1)}, u32[]{:S(2)}, u32[]{:S(2)}) async-start(f32[32,1,1280]{2,1,0:T(1,128)} %get-tuple-element.106), calls=%async_computation.3 | async-start | bytes 327680 | tf_op jit(solution)/shard_map/all_to_all | solution.py:827
where the time goes:
time: 70.9 us; the launch traced here: 70.4 us
  Pallas kernels  23.4 us (33%)
  starting transfers between devices  20 us (28%)
  waiting for transfers between devices  16 us (23%)
  blocking collectives  10.2 us (14%)
  between operations  0.74 us (1%)
    pallas_call x10, Pallas kernels, call(): run(*(pltpu.with_memory_space_constraint(arg, pltpu.HBM) if s == 'h' else...  23.4 us
    all_to_all x4, starting transfers between devices, exchange(): return lax.all_to_all(lines, axes, 0, 0, tiled=True).reshape(shape)  16.3 us
    all_to_all x4, waiting for transfers between devices, exchange(): return lax.all_to_all(lines, axes, 0, 0, tiled=True).reshape(shape)  16 us
    all_to_all x1, blocking collectives, exchange(): return lax.all_to_all(lines, axes, 0, 0, tiled=True).reshape(shape)  10.2 us
    ppermute x2, starting transfers between devices, beyond(): lax.ppermute(value, 'row', [(i + a, i + 1 - a) for i in range(start, z.pe...  3.67 us
  transfers between devices with their start and end apart: 6, of which 4 were waited for; matrix products, arithmetic and copies ran while one was open for 0% of the time, Pallas kernels for 18%

commit v1 on v0

--- a/solution.py
+++ b/solution.py
@@ -541,6 +541,9 @@
     fill_shifted(z, pads, above, below)
     columns = []
     for a in range(TAPS):
+        if a == 1:
+            columns.append(jnp.concatenate([own[:, :128], own[:, 128:]], axis=0))
+            continue
         columns.append(
             jnp.concatenate([pads[k][TAPS - 1 - a, h, pl.ds(z.step[k], z.count[k]), :] for h in (0, 1) for k in (1, 0)], axis=0)
         )

time: 70.9 us -> 70.9 us (level)
  no operation moved by 1% of the time
where the time goes in v1:
time: 70.9 us; the launch traced here: 70.4 us
  Pallas kernels  23.4 us (33%)
  starting transfers between devices  20 us (28%)
  waiting for transfers between devices  16 us (23%)
  blocking collectives  10.2 us (14%)
  between operations  0.74 us (1%)
    pallas_call x10, Pallas kernels, call(): run(*(pltpu.with_memory_space_constraint(arg, pltpu.HBM) if s == 'h' else...  23.4 us
    all_to_all x4, starting transfers between devices, exchange(): return lax.all_to_all(lines, axes, 0, 0, tiled=True).reshape(shape)  16.3 us
    all_to_all x4, waiting for transfers between devices, exchange(): return lax.all_to_all(lines, axes, 0, 0, tiled=True).reshape(shape)  16 us
    all_to_all x1, blocking collectives, exchange(): return lax.all_to_all(lines, axes, 0, 0, tiled=True).reshape(shape)  10.2 us
    ppermute x2, starting transfers between devices, beyond(): lax.ppermute(value, 'row', [(i + a, i + 1 - a) for i in range(start, z.pe...  3.67 us
  transfers between devices with their start and end apart: 6, of which 4 were waited for; matrix products, arithmetic and copies ran while one was open for 0% of the time, Pallas kernels for 18%

profile of v1, /device:TPU:0, one launch (start us, length us, event | category | flops | bytes accessed | tf_op | source)
XLA Modules:
  0.0 70.4 jit_solution(5409820630268588960)
XLA Ops:
  0.6 2.0 %shard_map.195 = (f32[256,256]{1,0:T(8,128)S(1)}, f32[248,256]{1,0:T(8,128)S(1)}, f32[248,256]{1,0:T(8,128)S(1)}, f32[64,128]{1,0:T(8,128)}) custom-call(f32[4,4,1024]{2,1,0:T(4,128)} %small.1, f32[3,8,2048]{2,1,0:T(8,128)} %large.1, f32[4,4,1024]{2,1,0:T(4,128)} %up_s.3, f32[3,8,2048]{2,1,0:T(8,128)} %up_l.3, f32[4,4,32]{2,1,0:T(4,128)} %t_s.3, f32[3,8,64]{2,1,0:T(8,128)} %t_l.3), custom_call_target="tpu_custom_call" | custom-call | tf_op jit(solution)/shard_map/pallas_call | solution.py:821
  2.6 3.0 %collective-permute-start = (f32[248,256]{1,0:T(8,128)S(1)}, f32[248,256]{1,0:T(8,128)S(1)}, u32[]{:S(2)}, u32[]{:S(2)}) collective-permute-start(f32[248,256]{1,0:T(8,128)S(1)} %get-tuple-element.68), channel_id=1, source_target_pairs={{0,1},{1,0},{2,3},{3,2},{4,5},{5,4},{6,7},{7,6},{8,9},{9,8},{10,11... | collective-permute-start | bytes 761864 | tf_op jit(solution)/shard_map/ppermute | solution.py:836
  5.6 0.7 collective-permute-start.1
  6.3 7.6 %all-to-all-start = ((f32[32,2,128]{2,1,0:T(2,128)}), f32[32,2,128]{2,1,0:T(2,128)S(1)}, u32[]{:S(2)}, u32[]{:S(2)}) async-start(f32[32,2,128]{2,1,0:T(2,128)} %bitcast), calls=%async_computation | async-start | bytes 65536 | tf_op jit(solution)/shard_map/all_to_all | solution.py:830
  13.9 2.8 %shard_map.196 = (bf16[2,576,128]{2,1,0:T(8,128)(2,1)S(1)}, bf16[2,576,128]{2,1,0:T(8,128)(2,1)S(1)}, bf16[3,2,576,128]{3,2,1,0:T(8,128)(2,1)}, f32[5,256]{1,0:T...) custom-call(f32[3,3,32,32]{3,2,1,0:T(8,128)} %first.1, f32[3,3,32,32]{3,2,1,0:T(8,128)} %second.1, ...), custom_call_target="tpu_custom_call" | custom-call | tf_op jit(solution)/shard_map/pallas_call | solution.py:821
  16.8 4.3 %all-to-all-done = f32[32,2,128]{2,1,0:T(2,128)S(1)} async-done(((f32[32,2,128]{2,1,0:T(2,128)}), f32[32,2,128]{2,1,0:T(2,128)S(1)}, u32[]{:S(2)}, u32[]{:S(2)}) %all-to-all-start) | async-done | bytes 32800 | tf_op jit(solution)/shard_map/all_to_all | solution.py:830
  21.1 0.0 collective-permute-done.pair
  21.1 0.0 collective-permute-done.1.other
  21.1 1.5 %shard_map.197 = (f32[256,256]{1,0:T(8,128)S(1)}, f32[2,256]{1,0:T(2,128)S(1)}, f32[64,128]{1,0:T(8,128)}) custom-call(f32[256,256]{1,0:T(8,128)S(1)} %get-tuple-element.67.x, f32[248,256]{1,0:T(8,128)S(1)} %collective-permute-done.pair, f32[248,256]{1,0:T(8,128)S(1)} %collective-permute-done.1.other, f32[64,128]{1,0:T(8,128)S(1)} %bitcast.16, ...), custom_call_target="tpu_custom_call" | custom-call | tf_op jit(solution)/shard_map/pallas_call | solution.py:821
  22.7 2.6 %all-to-all-start.1 = ((f32[32,2,128]{2,1,0:T(2,128)}), f32[32,2,128]{2,1,0:T(2,128)S(1)}, u32[]{:S(2)}, u32[]{:S(2)}) async-start(f32[32,2,128]{2,1,0:T(2,128)} %bitcast.6), calls=%async_computation.1 | async-start | bytes 65536 | tf_op jit(solution)/shard_map/all_to_all | solution.py:830
  25.3 4.3 %shard_map.198 = (f32[120,256]{1,0:T(8,128)S(1)}, f32[120,256]{1,0:T(8,128)S(1)}, bf16[2,256,512]{2,1,0:T(8,128)(2,1)}, f32[32,1280]{1,0:T(8,128)}, f32[416,256]...) custom-call(f32[256,256]{1,0:T(8,128)S(1)} %get-tuple-element.67.x, f32[256,256]{1,0:T(8,128)S(1)} %get-tuple-element.73.hidden, ...), custom_call_target="tpu_custom_call" | custom-call | tf_op jit(solution)/shard_map/pallas_call | solution.py:821
  29.6 2.8 %all-to-all-done.1 = f32[32,2,128]{2,1,0:T(2,128)S(1)} async-done(((f32[32,2,128]{2,1,0:T(2,128)}), f32[32,2,128]{2,1,0:T(2,128)S(1)}, u32[]{:S(2)}, u32[]{:S(2)}) %all-to-all-start.1) | async-done | bytes 32800 | tf_op jit(solution)/shard_map/all_to_all | solution.py:830
  32.4 1.8 %shard_map.199 = (f32[256,256]{1,0:T(8,128)S(1)}, f32[80,256]{1,0:T(8,128)S(1)}, f32[80,256]{1,0:T(8,128)S(1)}, f32[2,40,256]{2,1,0:T(8,128)S(1)}, f32[2,256]{1,0:T(2,128)S(1)}, /*index=5*/f32[64,128]{1,0:T(8,128)}) custom-call(f32[256,256]{1,0:T(8,128)S(1)} %get-tuple-element.73.hidden, f32[120,256]{1,0:T(8,128)S(1)} %get-tuple-element.78.h_above, ...), custom_call_target="tpu_custom_call" | custom-call | tf_op jit(solution)/shard_map/pallas_call | solution.py:821
  34.2 3.3 %all-to-all-start.2 = ((f32[8,8,128]{2,1,0:T(8,128)}), f32[8,8,128]{2,1,0:T(8,128)S(1)}, u32[]{:S(2)}, u32[]{:S(2)}) async-start(f32[8,8,128]{2,1,0:T(8,128)} %bitcast.8), calls=%async_computation.2 | async-start | bytes 65536 | tf_op jit(solution)/shard_map/all_to_all | solution.py:830
  37.6 3.7 %shard_map.200 = (f32[256,256]{1,0:T(8,128)}, f32[336,256]{1,0:T(8,128)}, bf16[2,256,512]{2,1,0:T(8,128)(2,1)S(1)}, f32[3,336,256]{2,1,0:T(8,128)}, f32[336,256]...) custom-call(f32[256,256]{1,0:T(8,128)S(1)} %get-tuple-element.73.hidden, ...), custom_call_target="tpu_custom_call" | custom-call | tf_op jit(solution)/shard_map/pallas_call | solution.py:821
  41.3 2.9 %all-to-all-done.2 = f32[8,8,128]{2,1,0:T(8,128)S(1)} async-done(((f32[8,8,128]{2,1,0:T(8,128)}), f32[8,8,128]{2,1,0:T(8,128)S(1)}, u32[]{:S(2)}, u32[]{:S(2)}) %all-to-all-start.2) | async-done | bytes 32800 | tf_op jit(solution)/shard_map/all_to_all | solution.py:830
  44.2 3.3 %shard_map.201 = (f32[256,256]{1,0:T(8,128)S(1)}, f32[256,256]{1,0:T(8,128)S(1)}, f32[40,256]{1,0:T(8,128)S(1)}, f32[40,256]{1,0:T(8,128)S(1)}, f32[32,1,1280]{2,1,0:T(1,128)}) custom-call(f32[64,128]{1,0:T(8,128)S(1)} %bitcast.14, f32[336,256]{1,0:T(8,128)S(1)} %get-tuple-element.96.up, f32[3,336,256]{2,1,0:T(8,128)} %get-tuple-element.97.shifts, ...), custom_call_target="tpu_custom_call" | custom-call | tf_op jit(solution)/shard_map/pallas_call | solution.py:821
  47.5 2.8 %all-to-all-start.3 = ((f32[32,1,1280]{2,1,0:T(1,128)}), f32[32,1,1280]{2,1,0:T(1,128)S(1)}, u32[]{:S(2)}, u32[]{:S(2)}) async-start(f32[32,1,1280]{2,1,0:T(1,128)} %get-tuple-element.106), calls=%async_computation.3 | async-start | bytes 327680 | tf_op jit(solution)/shard_map/all_to_all | solution.py:830
  50.3 2.0 %shard_map.202 = (f32[4,4,1024]{2,1,0:T(4,128)}, f32[3,8,2048]{2,1,0:T(8,128)}, f32[256,256]{1,0:T(8,128)S(1)}, f32[336,256]{1,0:T(8,128)S(1)}, bf16[2,576,128]{2,1,0:T(8,128)(2,1)S(1)}) custom-call(f32[256,256]{1,0:T(8,128)} %get-tuple-element.92.out, f32[256,256]{1,0:T(8,128)} %get-tuple-element.93.x, f32[336,256]{1,0:T(8,128)} %get-tuple-element.94.hidden, ...), custom_call_target="tpu_custom_call" | custom-call | tf_op jit(solution)/shard_map/pallas_call | solution.py:821
  52.3 5.9 %all-to-all-done.3.gathered = f32[32,1,1280]{2,1,0:T(1,128)S(1)} async-done(((f32[32,1,1280]{2,1,0:T(1,128)}), f32[32,1,1280]{2,1,0:T(1,128)S(1)}, u32[]{:S(2)}, u32[]{:S(2)}) %all-to-all-start.3) | async-done | bytes 163872 | tf_op jit(solution)/shard_map/all_to_all | solution.py:830
  58.2 0.9 %shard_map.203 = (f32[256,256]{1,0:T(8,128)S(1)}, f32[2,128]{1,0:T(2,128)S(1)}, f32[32,1,640]{2,1,0:T(1,128)S(1)}) custom-call(f32[32,1,1280]{2,1,0:T(1,128)S(1)} %all-to-all-done.3.gathered, f32[256,256]{1,0:T(8,128)S(1)} %get-tuple-element.107.dshift, f32[40,256]{1,0:T(8,128)S(1)} %get-tuple-element.103.order.d_above, ...), custom_call_target="tpu_custom_call" | custom-call | tf_op jit(solution)/shard_map/pallas_call | solution.py:821
  59.2 10.2 %all_to_all.25.gathered = f32[32,1,640]{2,1,0:T(1,128)S(1)} all-to-all(f32[32,1,640]{2,1,0:T(1,128)S(1)} %get-tuple-element.112), channel_id=1, replica_groups=mesh['img'=4,'row'=8] {'img','row'}, dimensions={0} | all-to-all | bytes 163840 | tf_op jit(solution)/shard_map/all_to_all | solution.py:830
  69.4 1.0 %shard_map.204 = (f32[4,4,1024]{2,1,0:T(4,128)}, f32[3,8,2048]{2,1,0:T(8,128)}, f32[3,3,32,32]{3,2,1,0:T(8,128)}, f32[3,3,32,32]{3,2,1,0:T(8,128)}, f32[1,32]{1,...) custom-call(f32[32,1,640]{2,1,0:T(1,128)S(1)} %all_to_all.25.gathered, ...), custom_call_target="tpu_custom_call" | custom-call | tf_op jit(solution)/shard_map/pallas_call | solution.py:821
Async XLA Ops:
  2.6 18.5 %collective-permute-start = (f32[248,256]{1,0:T(8,128)S(1)}, f32[248,256]{1,0:T(8,128)S(1)}, u32[]{:S(2)}, u32[]{:S(2)}) collective-permute-start(f32[248,256]{1,0:T(8,128)S(1)} %get-tuple-element.68), channel_id=1, source_target_pairs={{0,1},{1,0},{2,3},{3,2},{4,5},{5,4},{6,7},{7,6},{8,9},{9,8},{10,11... | collective-permute-start | bytes 761864 | tf_op jit(solution)/shard_map/ppermute | solution.py:836
  5.6 15.5 %collective-permute-start.1 = (f32[248,256]{1,0:T(8,128)S(1)}, f32[248,256]{1,0:T(8,128)S(1)}, u32[]{:S(2)}, u32[]{:S(2)}) collective-permute-start(f32[248,256]{1,0:T(8,128)S(1)} %get-tuple-element.69), channel_id=1, source_target_pairs={{1,2},{2,1},{3,4},{4,3},{5,6},{6,5},{9,10},{10,9},{11,12},{12,11},... | collective-permute-start | bytes 761864 | tf_op jit(solution)/shard_map/ppermute | solution.py:836
  6.3 14.8 %all-to-all-start = ((f32[32,2,128]{2,1,0:T(2,128)}), f32[32,2,128]{2,1,0:T(2,128)S(1)}, u32[]{:S(2)}, u32[]{:S(2)}) async-start(f32[32,2,128]{2,1,0:T(2,128)} %bitcast), calls=%async_computation | async-start | bytes 65536 | tf_op jit(solution)/shard_map/all_to_all | solution.py:830
  22.7 9.8 %all-to-all-start.1 = ((f32[32,2,128]{2,1,0:T(2,128)}), f32[32,2,128]{2,1,0:T(2,128)S(1)}, u32[]{:S(2)}, u32[]{:S(2)}) async-start(f32[32,2,128]{2,1,0:T(2,128)} %bitcast.6), calls=%async_computation.1 | async-start | bytes 65536 | tf_op jit(solution)/shard_map/all_to_all | solution.py:830
  34.2 10.0 %all-to-all-start.2 = ((f32[8,8,128]{2,1,0:T(8,128)}), f32[8,8,128]{2,1,0:T(8,128)S(1)}, u32[]{:S(2)}, u32[]{:S(2)}) async-start(f32[8,8,128]{2,1,0:T(8,128)} %bitcast.8), calls=%async_computation.2 | async-start | bytes 65536 | tf_op jit(solution)/shard_map/all_to_all | solution.py:830
  47.5 10.7 %all-to-all-start.3 = ((f32[32,1,1280]{2,1,0:T(1,128)}), f32[32,1,1280]{2,1,0:T(1,128)S(1)}, u32[]{:S(2)}, u32[]{:S(2)}) async-start(f32[32,1,1280]{2,1,0:T(1,128)} %get-tuple-element.106), calls=%async_computation.3 | async-start | bytes 327680 | tf_op jit(solution)/shard_map/all_to_all | solution.py:830
